TPU v7x, 512 devices: a whole 4x4x16 slice. The times are simulated.
512 devices in a mesh: seq: 32 (over z_hi, x, core), head: 16 (over z_lo, y).
Axes of the slice: x: 4, y: 4, z: 16 (z_hi: 4, z_lo: 4; z = z_hi * 4 + z_lo), core: 2. Of those that a mesh axis runs over, the one named last changes fastest.
Arguments:
- query_rows: bfloat16 [4096, 2048], P('seq', 'head'), may hold values from -6 to 6
- key_rows: bfloat16 [4096, 128], P('seq'), may hold values from -6 to 6
- value_rows: bfloat16 [4096, 128], P('seq'), may hold values from -6 to 6
- out_grad: bfloat16 [4096, 2048], P('seq', 'head'), may hold values from -3 to 3
Outputs:
- attended: bfloat16 [4096, 2048], P('seq', 'head')
- query_grad: bfloat16 [4096, 2048], P('seq', 'head')
- key_grad: bfloat16 [4096, 128], P('seq')
- value_grad: bfloat16 [4096, 128], P('seq')
All inputs are finite; a program needn't handle non-finite values.
Results may differ from a plain program's by a relative error of at most 0.023.
Values may be sent and summed in bfloat16 or wider, within the bound.
A program may use at most 64 MiB of HBM per device.

v0:
```python
import jax
import jax.numpy as jnp
import numpy as np
from jax import lax
from jax.sharding import Mesh
from jax.sharding import PartitionSpec as P

SEQ = ("seq_0", "seq_1", "seq_2")


EPSILON = 1e-06


def filled_with(shard, identity):
    return jnp.zeros_like(shard) + jnp.asarray(identity, shard.dtype)


def carried_in(shard, axes, combine, identity):
    before = start = filled_with(shard, identity)
    running = shard
    for axis in reversed(axes):
        length, here = (lax.axis_size(axis), lax.axis_index(axis))
        pieces = lax.all_gather(running, axis)
        inside, running = (start, start)
        for k in range(length):
            passed = k < here
            running = combine(running, pieces[k])
            inside = jnp.where(passed, running, inside)
        before = combine(inside, before)
    return before


def laid_out(pieces, dim):
    pieces = jnp.moveaxis(pieces, 0, dim)
    dims = pieces.shape
    return pieces.reshape(*dims[:dim], dims[dim] * dims[dim + 1], *dims[dim + 2 :])


def copy_for_each(shard, axis):
    length = lax.axis_size(axis)
    return lax.all_to_all(
        jnp.broadcast_to(shard[None], (length, *shard.shape)), axis, 0, 0, tiled=True
    )


def gather_directly(shard, axis, dim):
    return laid_out(copy_for_each(shard, axis), dim)


def cut_along(shard, dim, length):
    dims = shard.shape
    pieces = shard.reshape(*dims[:dim], length, dims[dim] // length, *dims[dim + 1 :])
    return jnp.moveaxis(pieces, dim, 0)


def sum_at_owner(shard, axis, dim):
    pieces = cut_along(shard, dim, lax.axis_size(axis))
    arrived = lax.all_to_all(pieces, axis, split_axis=0, concat_axis=0, tiled=True)
    return arrived.astype(jnp.float32).sum(axis=0)


def entering(shard, axes, combine, identity):
    before = start = filled_with(shard, identity)
    running = shard
    for axis in reversed(axes):
        length, here = (lax.axis_size(axis), lax.axis_index(axis))
        pieces = lax.all_gather(running.astype(jnp.bfloat16), axis)
        inside, running = (start, start)
        for k in reversed(range(length)):
            passed = k > here
            running = combine(running, pieces[k].astype(shard.dtype))
            inside = jnp.where(passed, running, inside)
        before = combine(inside, before)
    return before


def pair_tables(head_width):
    first_index, second_index = np.triu_indices(head_width)
    return (jnp.asarray(first_index, dtype=jnp.int32), jnp.asarray(second_index, dtype=jnp.int32))


def picker(picked, head_width):
    return (jnp.arange(head_width, dtype=jnp.int32)[:, None] == picked[None, :]).astype(
        jnp.bfloat16
    )


def columns(source, picked):
    return jnp.dot(source, picker(picked, source.shape[-1]), preferred_element_type=jnp.float32)


def multiplicity(first_index, second_index):
    return jnp.where(first_index == second_index, 1.0, 2.0).astype(jnp.float32)


def query_features(source, first_index, second_index):
    expanded = columns(source, first_index) * columns(source, second_index)
    return (expanded * multiplicity(first_index, second_index)).astype(jnp.bfloat16)


def selector(picked, head_width):
    return (picked[:, None] == jnp.arange(head_width, dtype=jnp.int32)[None, :]).astype(
        jnp.bfloat16
    )


def spread_back(coeffs, source, first_index, second_index):
    head_width = source.shape[-1]
    left_terms = (coeffs * columns(source, second_index)).astype(jnp.bfloat16)
    right_terms = (coeffs * columns(source, first_index)).astype(jnp.bfloat16)
    summed = jnp.dot(
        left_terms, selector(first_index, head_width), preferred_element_type=jnp.float32
    )
    return summed + jnp.dot(
        right_terms, selector(second_index, head_width), preferred_element_type=jnp.float32
    )


def contract_rows(left_side, right_side):
    return lax.dot_general(
        left_side, right_side, (((0,), (0,)), ((), ())), preferred_element_type=jnp.float32
    )


def contract_last(left_side, right_side):
    return lax.dot_general(
        left_side, right_side, (((1,), (1,)), ((), ())), preferred_element_type=jnp.float32
    )


def over_blocks(running_sum, shard_piece, offset, block_size, update):

    def inner_step(position, carried):
        sub_block = lax.dynamic_slice_in_dim(shard_piece, position * block_size, block_size)
        return update(carried, sub_block, offset + position * block_size)

    return lax.fori_loop(0, shard_piece.shape[0] // block_size, inner_step, running_sum)


def local(query_rows, key_rows, value_rows, out_grad):
    row_count, head_width = key_rows.shape
    heads_here = query_rows.shape[1] // head_width
    feat_here = head_width * (head_width + 1) // 2 // lax.axis_size("head")
    first_all, second_all = pair_tables(head_width)
    offset = lax.axis_index("head") * feat_here
    first_mine = lax.dynamic_slice_in_dim(first_all, offset, feat_here)
    second_mine = lax.dynamic_slice_in_dim(second_all, offset, feat_here)
    group_rows = heads_here * row_count
    stacked_query = (
        query_rows.reshape(row_count, heads_here, head_width)
        .transpose(1, 0, 2)
        .reshape(group_rows, head_width)
    )
    stacked_grad = (
        out_grad.reshape(row_count, heads_here, head_width)
        .transpose(1, 0, 2)
        .reshape(group_rows, head_width)
    )
    key_features = (columns(key_rows, first_mine) * columns(key_rows, second_mine)).astype(
        jnp.bfloat16
    )
    local_state = contract_rows(key_features, value_rows)
    prefix = carried_in(local_state, SEQ, jnp.add, jnp.zeros_like(local_state)).astype(jnp.bfloat16)
    whole_state = gather_directly(prefix, "head", 0)
    zero_rows = jnp.zeros((group_rows, head_width), jnp.float32)
    query_heads = stacked_query.reshape(heads_here, row_count, head_width)
    places = jnp.arange(row_count, dtype=jnp.int32)
    causal = places[:, None] >= places[None, :]
    products = jnp.einsum("hrd,sd->hrs", query_heads, key_rows, preferred_element_type=jnp.float32)
    weights = jnp.where(causal, products * products, 0.0).astype(jnp.bfloat16)
    local_part = jnp.einsum(
        "hrs,sd->hrd", weights, value_rows, preferred_element_type=jnp.float32
    ).reshape(group_rows, head_width)
    all_query = gather_directly(stacked_query, "head", 0)

    def one_group(position):
        picked = lax.dynamic_slice_in_dim(all_query, position * group_rows, group_rows)
        features = query_features(picked, first_mine, second_mine)
        return jnp.dot(features, prefix, preferred_element_type=jnp.float32)

    groups = lax.map(
        one_group, jnp.arange(group_rows * lax.axis_size("head") // group_rows, dtype=jnp.int32)
    )
    remote_part = sum_at_owner(
        groups.reshape(group_rows * lax.axis_size("head"), head_width).astype(jnp.bfloat16),
        "head",
        0,
    )
    numerator = local_part + remote_part
    root_mean = jnp.sqrt(jnp.mean(numerator * numerator, axis=-1, keepdims=True) + EPSILON)
    normed = numerator / root_mean
    attended = (
        normed.astype(jnp.bfloat16)
        .reshape(heads_here, row_count, head_width)
        .transpose(1, 0, 2)
        .reshape(row_count, group_rows // row_count * head_width)
    )
    grad_float = stacked_grad.astype(jnp.float32)
    numer_grad = (
        (grad_float - normed * jnp.mean(grad_float * normed, axis=-1, keepdims=True)) / root_mean
    ).astype(jnp.bfloat16)
    grad_heads = numer_grad.reshape(heads_here, row_count, head_width)
    value_dots = jnp.einsum(
        "hrd,sd->hrs", grad_heads, value_rows, preferred_element_type=jnp.float32
    )
    coefficient = jnp.where(causal, 2.0 * products * value_dots, 0.0).astype(jnp.bfloat16)
    query_local = jnp.einsum(
        "hrs,sd->hrd", coefficient, key_rows, preferred_element_type=jnp.float32
    ).reshape(group_rows, head_width)
    key_local = jnp.einsum(
        "hrs,hrd->sd", coefficient, query_heads, preferred_element_type=jnp.float32
    )
    value_local = jnp.einsum("hrs,hrd->sd", weights, grad_heads, preferred_element_type=jnp.float32)

    def add_query_grad(summed, sub_block, start_feature):
        first_index = lax.dynamic_slice_in_dim(first_all, start_feature, sub_block.shape[0])
        second_index = lax.dynamic_slice_in_dim(second_all, start_feature, sub_block.shape[0])
        coeffs = contract_last(numer_grad, sub_block) * multiplicity(first_index, second_index)
        return summed + spread_back(coeffs, stacked_query, first_index, second_index)

    remote_grad = over_blocks(zero_rows, whole_state, 0, feat_here, add_query_grad)
    query_grad = (
        (query_local + remote_grad)
        .astype(jnp.bfloat16)
        .reshape(heads_here, row_count, head_width)
        .transpose(1, 0, 2)
        .reshape(row_count, group_rows // row_count * head_width)
    )
    all_grad = gather_directly(numer_grad, "head", 0)

    def add_dual(position, summed):
        picked_query = lax.dynamic_slice_in_dim(all_query, position * row_count, row_count)
        picked_grad = lax.dynamic_slice_in_dim(all_grad, position * row_count, row_count)
        features = query_features(picked_query, first_mine, second_mine)
        return summed + contract_rows(features, picked_grad)

    dual_local = lax.fori_loop(
        0, all_query.shape[0] // row_count, add_dual, jnp.zeros_like(local_state)
    )
    suffix = entering(dual_local, SEQ, jnp.add, jnp.zeros_like(dual_local)).astype(jnp.bfloat16)
    key_coeffs = contract_last(value_rows, suffix)
    key_part = key_local + spread_back(key_coeffs, key_rows, first_mine, second_mine)
    value_part = value_local + jnp.dot(key_features, suffix, preferred_element_type=jnp.float32)
    key_sum, value_sum = (
        lax.psum(key_part.astype(jnp.bfloat16), "head").astype(jnp.float32),
        lax.psum(value_part.astype(jnp.bfloat16), "head").astype(jnp.float32),
    )
    return (attended, query_grad, key_sum.astype(jnp.bfloat16), value_sum.astype(jnp.bfloat16))


def solution(mesh):
    torus = Mesh(
        mesh.devices.reshape(4, 4, 2, mesh.shape["head"]), ("seq_0", "seq_1", "seq_2", "head")
    )
    return jax.shard_map(
        local,
        mesh=torus,
        in_specs=(P(SEQ, "head"), P(SEQ, None), P(SEQ, None), P(SEQ, "head")),
        out_specs=(P(SEQ, "head"), P(SEQ, "head"), P(SEQ, None), P(SEQ, None)),
        check_vma=False,
    )
```

profile of v0, /device:TPU:6, one launch (start us, length us, event | category | flops | bytes accessed | tf_op | source)
XLA Modules:
  0.0 473.0 jit_solution(7803446797328281559)
XLA Ops:
  11.7 2.2 all-gather.3
  15.5 8.6 %all-to-all-start = ((bf16[16,128,128]{2,1,0:T(8,128)(2,1)}), bf16[16,128,128]{2,1,0:T(8,128)(2,1)S(1)}, u32[]{:S(2)}, u32[]{:S(2)}) async-start(bf16[16,128,128]{2,1,0:T(8,128)(2,1)} %broadcast_in_dim.127), calls=%async_computation | async-start | bytes 1048576 | tf_op jit(solution)/shard_map/all_to_all | solution.py:41
  24.2 25.6 %all-gather.11.cloned.1.call-done = f32[4,516,128]{2,1,0:T(8,128)} async-done(((f32[1,516,128]{2,1,0:T(8,128)}), f32[4,516,128]{2,1,0:T(8,128)}) %all-gather.11.cloned.1.call-update) | async-done | bytes 1056784 | tf_op jit(solution)/shard_map/all_gather | solution.py:23
  49.8 2.1 slice_add_fusion.3
  52.7 62.3 %all-gather.9.cloned.1.call-done = f32[4,516,128]{2,1,0:T(8,128)} async-done(((f32[1,516,128]{2,1,0:T(8,128)}), f32[4,516,128]{2,1,0:T(8,128)}) %all-gather.9.cloned.1.call-update) | async-done | bytes 1056784 | tf_op jit(solution)/shard_map/all_gather | solution.py:23
  115.0 1.4 fusion.87
  116.4 42.8 %while.41 = (s32[]{:T(128)}, bf16[16,128,128]{2,1,0:T(8,128)(2,1)}, s32[16]{0:T(128)S(1)}, bf16[2048,128]{1,0:T(8,128)(2,1)S(1)}, s32[516]{0:T(1024)S(1)}, /*ind...) while((s32[]{:T(128)}, bf16[16,128,128]{2,1,0:T(8,128)(2,1)}, ...), condition=%wide.region_1.2_spmd, body=%wide.region_0.1_spmd.sunk | while | flops 51055624 | bytes 810187 | solution.py:181
  159.3 5.7 %all-to-all-start.1 = ((bf16[16,128,128]{2,1,0:T(8,128)(2,1)}), bf16[16,128,128]{2,1,0:T(8,128)(2,1)S(1)}, u32[]{:S(2)}, u32[]{:S(2)}) async-start(bf16[16,128,128]{2,1,0:T(8,128)(2,1)} %get-tuple-element.338), calls=%async_computation.1 | async-start | bytes 1048576 | tf_op jit(solution)/shard_map/all_to_all | solution.py:58
  165.2 15.4 %all-to-all-done.1 = bf16[16,128,128]{2,1,0:T(8,128)(2,1)S(1)} async-done(((bf16[16,128,128]{2,1,0:T(8,128)(2,1)}), bf16[16,128,128]{2,1,0:T(8,128)(2,1)S(1)}, u32[]{:S(2)}, u32[]{:S(2)}) %all-to-all-start.1) | async-done | bytes 524320 | tf_op jit(solution)/shard_map/all_to_all | solution.py:58
  182.1 4.5 all-to-all-start.3
  189.2 12.1 %all-to-all-done.3 = bf16[16,128,128]{2,1,0:T(8,128)(2,1)S(1)} async-done(((bf16[16,128,128]{2,1,0:T(8,128)(2,1)}), bf16[16,128,128]{2,1,0:T(8,128)(2,1)S(1)}, u32[]{:S(2)}, u32[]{:S(2)}) %all-to-all-start.3) | async-done | bytes 524320 | tf_op jit(solution)/shard_map/all_to_all | solution.py:41
  201.3 1.6 broadcast_in_dim.129
  202.9 4.4 all-to-all-start.2
  207.4 56.2 %while.42 = (s32[]{:T(128)}, f32[516,128]{1,0:T(8,128)S(1)}, bf16[2048,128]{1,0:T(8,128)(2,1)S(1)}, s32[516]{0:T(1024)}, s32[516]{0:T(1024)S(1)}, /*index=5*/pre...) while((s32[]{:T(128)}, f32[516,128]{1,0:T(8,128)S(1)}, ...), condition=%wide.region_8.9_spmd.clone, body=%wide.region_7.8_spmd.clone.sunk | while | flops 51187720 | bytes 1173708 | solution.py:237
  208.4 1.3 select_reduce_fusion.5
  211.9 1.3 select_reduce_fusion.5
  263.6 2.1 all-gather.5
  265.8 13.5 %all_gather.34 = bf16[4,516,128]{2,1,0:T(8,128)(2,1)S(1)} all-gather(bf16[1,516,128]{2,1,0:T(8,128)(2,1)S(1)} %fusion.73), channel_id=1, replica_groups=mesh['seq_0'=4,'seq_1'=4,'seq_2'=2,'head'=16] {'seq_1'}, dimensions={0}, use_global_device_ids=true | all-gather | bytes 660480 | tf_op jit(solution)/shard_map/all_gather | solution.py:67
  279.4 26.5 %all_gather.35 = bf16[4,516,128]{2,1,0:T(8,128)(2,1)S(1)} all-gather(bf16[1,516,128]{2,1,0:T(8,128)(2,1)S(1)} %fusion.74), channel_id=1, replica_groups=mesh['seq_0'=4,'seq_1'=4,'seq_2'=2,'head'=16] {'seq_0'}, dimensions={0}, use_global_device_ids=true | all-gather | bytes 660480 | tf_op jit(solution)/shard_map/all_gather | solution.py:67
  308.6 2.0 reshape.176
  310.7 73.3 %while.43 = (s32[]{:T(128)}, f32[128,128]{1,0:T(8,128)S(1)}, bf16[8256,128]{1,0:T(8,128)(2,1)}, bf16[128,128]{1,0:T(8,128)(2,1)S(1)}, bf16[128,128]{1,0:T(8,128)...) while((s32[]{:T(128)}, f32[128,128]{1,0:T(8,128)S(1)}, ...), condition=%wide.region_6.7_spmd.clone.clone, body=%wide.region_5.6_spmd.sunk.clone.clone.sunk | while | flops 85318160 | bytes 1311093 | solution.py:137
  384.7 79.0 %all-reduce.3.cloned.1.call-done = (bf16[128,128]{1,0:T(8,128)(2,1)}, bf16[128,128]{1,0:T(8,128)(2,1)}) async-done(((bf16[128,128]{1,0:T(8,128)(2,1)}, bf16[128,128]{1,0:T(8,128)(2,1)}), (bf16[128,128]{1,0:T(8,128)(2,1)}, bf16[128,128]{1,0:T(8,128)(2,1)})) %all-reduce.3.cloned.1.call-update) | async-done | bytes 65552 | tf_op jit(solution)/shard_map/psum | solution.py:245
  463.8 1.4 copy.44
  465.1 1.4 copy.45
  (287 shorter events, 172.7 us)
Async XLA Ops:
  7.2 1.6 copy-start
  7.2 7.4 %copy-start.1 = (bf16[128,128]{1,0:T(8,128)(2,1)S(1)}, bf16[128,128]{1,0:T(8,128)(2,1)}, u32[]{:S(2)}) copy-start(bf16[128,128]{1,0:T(8,128)(2,1)} %param.12) | copy-start | bytes 98308
  7.2 42.6 %all-gather.11.cloned.1.call-start = ((), (), s32[]{:S(2)}) async-start(), calls=%async_computation.5 | async-start | bytes 1331200 | tf_op jit(solution)/shard_map/all_gather | solution.py:23
  15.5 100.9 %all-to-all-start = ((bf16[16,128,128]{2,1,0:T(8,128)(2,1)}), bf16[16,128,128]{2,1,0:T(8,128)(2,1)S(1)}, u32[]{:S(2)}, u32[]{:S(2)}) async-start(bf16[16,128,128]{2,1,0:T(8,128)(2,1)} %broadcast_in_dim.127), calls=%async_computation | async-start | bytes 1048576 | tf_op jit(solution)/shard_map/all_to_all | solution.py:41
  24.2 90.8 %all-gather.9.cloned.1.call-start = ((), (), s32[]{:S(2)}) async-start(), calls=%async_computation.4 | async-start | bytes 1331200 | tf_op jit(solution)/shard_map/all_gather | solution.py:23
  49.8 65.2 %copy-start.2 = (f32[4,516,128]{2,1,0:T(8,128)S(1)}, f32[4,516,128]{2,1,0:T(8,128)}, u32[]{:S(2)}) copy-start(f32[4,516,128]{2,1,0:T(8,128)} %all-gather.11.cloned.1.call-done) | copy-start | bytes 3170308
  116.4 48.5 %copy-start.17 = (bf16[128,128]{1,0:T(8,128)(2,1)S(1)}, bf16[128,128]{1,0:T(8,128)(2,1)}, u32[]{:S(2)}) copy-start(bf16[128,128]{1,0:T(8,128)(2,1)} %param.15) | copy-start | bytes 98308
  116.4 64.3 %copy-start.10 = (bf16[128,128]{1,0:T(8,128)(2,1)S(1)}, bf16[128,128]{1,0:T(8,128)(2,1)}, u32[]{:S(2)}) copy-start(bf16[128,128]{1,0:T(8,128)(2,1)} %param.14) | copy-start | bytes 98308
  159.2 21.8 %copy-start.8 = (s32[516]{0:T(1024)}, s32[516]{0:T(1024)S(1)}, u32[]{:S(2)}) copy-start(s32[516]{0:T(1024)S(1)} %get-tuple-element.729) | copy-start | bytes 6196
  159.3 21.8 %copy-start.12 = (pred[1,516]{1,0:T(4,128)(4,1)}, pred[1,516]{1,0:T(4,128)(4,1)S(1)}, u32[]{:S(2)}) copy-start(pred[1,516]{1,0:T(4,128)(4,1)S(1)} %get-tuple-element.731) | copy-start | bytes 1552
  159.3 21.3 %all-to-all-start.1 = ((bf16[16,128,128]{2,1,0:T(8,128)(2,1)}), bf16[16,128,128]{2,1,0:T(8,128)(2,1)S(1)}, u32[]{:S(2)}, u32[]{:S(2)}) async-start(bf16[16,128,128]{2,1,0:T(8,128)(2,1)} %get-tuple-element.338), calls=%async_computation.1 | async-start | bytes 1048576 | tf_op jit(solution)/shard_map/all_to_all | solution.py:58
  182.1 19.2 %all-to-all-start.3 = ((bf16[16,128,128]{2,1,0:T(8,128)(2,1)}), bf16[16,128,128]{2,1,0:T(8,128)(2,1)S(1)}, u32[]{:S(2)}, u32[]{:S(2)}) async-start(bf16[16,128,128]{2,1,0:T(8,128)(2,1)} %broadcast_in_dim.130), calls=%async_computation.3 | async-start | bytes 1048576 | tf_op jit(solution)/shard_map/all_to_all | solution.py:41
  187.6 15.3 %copy-start.13 = (bf16[128,128]{1,0:T(8,128)(2,1)}, bf16[128,128]{1,0:T(8,128)(2,1)S(1)}, u32[]{:S(2)}) copy-start(bf16[128,128]{1,0:T(8,128)(2,1)S(1)} %fusion.52) | copy-start | bytes 98308
  201.3 1.6 copy-start.7
  202.9 105.7 %all-to-all-start.2 = ((bf16[16,516,128]{2,1,0:T(8,128)(2,1)}), bf16[16,516,128]{2,1,0:T(8,128)(2,1)S(1)}, u32[]{:S(2)}, u32[]{:S(2)}) async-start(bf16[16,516,128]{2,1,0:T(8,128)(2,1)} %broadcast_in_dim.129), calls=%async_computation.2 | async-start | bytes 4259840 | tf_op jit(solution)/shard_map/all_to_all | solution.py:41
  207.3 256.4 %all-reduce.3.cloned.1.call-start = ((), (), s32[]{:S(2)}) async-start(), calls=%async_computation.6 | async-start | bytes 131072 | tf_op jit(solution)/shard_map/psum | solution.py:245
  263.6 42.5 %copy-start.5 = (bf16[516,128]{1,0:T(8,128)(2,1)S(1)}, bf16[516,128]{1,0:T(8,128)(2,1)}, u32[]{:S(2)}) copy-start(bf16[516,128]{1,0:T(8,128)(2,1)} %copy-done.4) | copy-start | bytes 396292
  263.6 42.5 %copy-start.15 = (f32[128,128]{1,0:T(8,128)S(1)}, f32[128,128]{1,0:T(8,128)}, u32[]{:S(2)}) copy-start(f32[128,128]{1,0:T(8,128)} %fusion.91) | copy-start | bytes 196612
  265.8 41.3 %copy-start.11 = (bf16[128,128]{1,0:T(8,128)(2,1)S(1)}, bf16[128,128]{1,0:T(8,128)(2,1)}, u32[]{:S(2)}) copy-start(bf16[128,128]{1,0:T(8,128)(2,1)} %param.14) | copy-start | bytes 98308
  265.8 41.4 %copy-start.9 = (s32[516]{0:T(1024)S(1)}, s32[516]{0:T(1024)}, u32[]{:S(2)}) copy-start(s32[516]{0:T(1024)} %get-tuple-element.730) | copy-start | bytes 6196
  279.4 28.3 %copy-start.6 = (f32[516,128]{1,0:T(8,128)S(1)}, f32[516,128]{1,0:T(8,128)}, u32[]{:S(2)}) copy-start(f32[516,128]{1,0:T(8,128)} %get-tuple-element.475) | copy-start | bytes 792580
  279.4 28.3 %copy-start.16 = (f32[128,128]{1,0:T(8,128)S(1)}, f32[128,128]{1,0:T(8,128)}, u32[]{:S(2)}) copy-start(f32[128,128]{1,0:T(8,128)} %fusion.96) | copy-start | bytes 196612
  308.6 2.1 copy-start.3
  310.7 73.3 %copy-start.14 = (bf16[128,128]{1,0:T(8,128)(2,1)S(1)}, bf16[128,128]{1,0:T(8,128)(2,1)}, u32[]{:S(2)}) copy-start(bf16[128,128]{1,0:T(8,128)(2,1)} %copy-done.13) | copy-start | bytes 98308
  (1 other events, 0.7 us)
Sparse Core Ops, SparseCore 0:
  14.7 34.9 all-gather.10
  52.0 62.9 all-gather.8
  308.7 154.9 all-reduce.2
where the time goes:
time: 479 us; the launch traced here: 473 us
  waiting for transfers between devices  194 us (41%)
  matrix products  100 us (21%)
  local copies, waits for them, and re-layouts  45.7 us (10%)
  blocking collectives  44.3 us (9%)
  other arithmetic  39.2 us (8%)
  starting transfers between devices  23.3 us (5%)
  between operations  14.2 us (3%)
  loops' own time  12 us (3%)
    all_gather x2, waiting for transfers between devices, carried_in(): pieces = lax.all_gather(running, axis)  87.8 us
    psum x1, waiting for transfers between devices, local(): lax.psum(key_part.astype(jnp.bfloat16), 'head').astype(jnp.float32)  79 us
    all_gather x3, blocking collectives, entering(): pieces = lax.all_gather(running.astype(jnp.bfloat16), axis)  42.1 us
    select_n x48, other arithmetic, multiplicity(): return jnp.where(first_index == second_index, 1.0, 2.0).astype(jnp.float32)  33.6 us
    dot_general x34, matrix products, columns(): jnp.dot(source, picker(picked, source.shape[-1]), preferred_element_type=...  20.8 us
    dot_general x17, matrix products, contract_rows(): lax.dot_general(left_side, right_side, (((0,), (0,)), ((), ())), preferre...  20.8 us
    dot_general x17, matrix products, contract_last(): lax.dot_general(left_side, right_side, (((1,), (1,)), ((), ())), preferre...  18.5 us
    dot_general x16, matrix products, one_group(): return jnp.dot(features, prefix, preferred_element_type=jnp.float32)  18.1 us
  transfers between devices with their start and end apart: 7, of which 5 were waited for; matrix products, arithmetic and copies ran while one was open for 30% of the time, Pallas kernels for 0%

commit v1 on v0

v1 whole, which is shorter than its diff:
```python
import jax
import jax.numpy as jnp
from jax import lax
from jax.experimental import pallas as pl
from jax.experimental.pallas import tpu as pltpu
from jax.sharding import PartitionSpec as P

MESH = pl.DeviceIdType.MESH
EPSILON = 1e-06
BF = jnp.bfloat16
F32 = jnp.float32
ROWS = 128
D = 128
ORDER = (0, 1, 3, 2)
BACK = (2, 1, 3, 0)


def dot_last(a, b):
    return lax.dot_general(a, b, (((1,), (1,)), ((), ())), preferred_element_type=F32)


def dot_first(a, b):
    return lax.dot_general(a, b, (((0,), (0,)), ((), ())), preferred_element_type=F32)


def dot(a, b):
    return jnp.dot(a, b, preferred_element_type=F32)


def kernel(
    q_in, k_in, v_in, g_in,
    att_ref, dq_ref, dkv_ref,
    qall, ngall, gbuf, kv, s_ref, w_ref, part, parts, partr,
    dqacc, dqs, dqr, dkvs, yr, zs, zr, fin,
    lsem, zsem, zrsem, csem, qsem, qrsem, fsem, frsem,
    nsem, nrsem, gsem, grsem, dsem, drsem, ysem, yrsem, asem, arsem, osem, orsem,
):
    seq, head = lax.axis_index("seq"), lax.axis_index("head")
    zhi, x, core = seq // 8, (seq // 2) % 4, seq % 2
    zlo, y = head // 4, head % 4

    def dev(dzhi=0, dx=0, dcore=0, dzlo=0, dy=0):
        return (
            (((zhi + dzhi) % 4) * 4 + (x + dx) % 4) * 2 + (core + dcore) % 2,
            ((zlo + dzlo) % 4) * 4 + (y + dy) % 4,
        )

    peers = [dev(dx=e) for e in (1, 2, 3)]
    peers += [dev(dcore=r, dy=f) for r in (0, 1) for f in range(4) if (r, f) != (0, 0)]
    peers += [dev(dzhi=d, dzlo=m) for d in range(4) for m in range(4) if (d, m) != (0, 0)]
    peers += [dev(dy=f, dzlo=m) for f in (1, 2, 3) for m in (1, 2, 3)]
    barrier = pltpu.get_barrier_semaphore()
    for p in peers:
        pl.semaphore_signal(barrier, 1, device_id=p, device_id_type=MESH)
    loads = [
        pltpu.make_async_copy(k_in, kv.at[0, 0, 0], lsem.at[0]),
        pltpu.make_async_copy(v_in, kv.at[0, 0, 1], lsem.at[1]),
        pltpu.make_async_copy(q_in, qall.at[0], lsem.at[2]),
        pltpu.make_async_copy(g_in, gbuf, lsem.at[3]),
    ]
    for c in loads:
        c.start()
    for c in loads:
        c.wait()
    pl.semaphore_wait(barrier, len(peers))

    sent = []

    def send(src, dst, ssem, rsem, to):
        c = pltpu.make_async_remote_copy(
            src_ref=src, dst_ref=dst, send_sem=ssem, recv_sem=rsem, device_id=to, device_id_type=MESH
        )
        c.start()
        sent.append(c)
        return c

    mine = pl.ds(pl.multiple_of(y * 32, 32), 32)
    from_z = {}
    for d in (2, 1, 3):
        from_z[d] = send(
            kv.at[0, 0, :, mine, :], kv.at[d, 0, :, mine, :], zsem.at[d - 1], zrsem.at[d - 1], dev(dzhi=d)
        )
    from_core = send(kv.at[0, 0], kv.at[0, 1], csem.at[0], csem.at[1], dev(dcore=1))
    from_x = [
        send(qall.at[0], qall.at[4 - e], qsem.at[e - 1], qrsem.at[e - 1], dev(dx=e)) for e in (1, 2, 3)
    ]

    gap = lax.broadcasted_iota(jnp.int32, (ROWS, ROWS), 1) - lax.broadcasted_iota(
        jnp.int32, (ROWS, ROWS), 0
    )

    def forward(d):
        queries = qall[...].reshape(4 * ROWS, D)
        keys = kv[d, :, 0].reshape(2 * ROWS, D)
        values = kv[d, :, 1].reshape(2 * ROWS, D)
        products = dot_last(queries, keys)
        for e in range(4):
            block = (zhi * 4 + (x + e) % 4) * 2 + core
            for r in range(2):
                other = (((zhi + 4 - d) % 4) * 4 + x) * 2 + (core + r) % 2
                tile = products[e * ROWS : (e + 1) * ROWS, r * ROWS : (r + 1) * ROWS]
                tile = jnp.where(gap <= (block - other) * ROWS, tile, 0.0)
                s_ref[d, pl.ds(e * ROWS, ROWS), pl.ds(r * ROWS, ROWS)] = tile
                w_ref[d, pl.ds(e * ROWS, ROWS), pl.ds(r * ROWS, ROWS)] = (tile * tile).astype(BF)
        return dot(w_ref[d], values)

    from_core.wait_recv()
    for c in from_x:
        c.wait_recv()
    part[...] = forward(0)
    from_y = {}
    for d in ORDER[1:]:
        from_z[d].wait_recv()
        from_y[d] = []
        for r in (0, 1):
            for f in range(4):
                if (r, f) != (0, 0):
                    from_y[d].append(
                        send(
                            kv.at[d, 0, :, mine, :], kv.at[d, r, :, mine, :],
                            fsem.at[d - 1, r * 4 + f], frsem.at[d - 1, r * 4 + f], dev(dcore=r, dy=f),
                        )
                    )
    for d in ORDER[1:]:
        for c in from_y[d]:
            c.wait_recv()
        part[...] += forward(d)

    arrivals = []
    for e in (2, 1, 3):
        parts[e - 1] = part[pl.ds(e * ROWS, ROWS), :].astype(BF)
        arrivals.append(send(parts.at[e - 1], partr.at[e - 1], nsem.at[e - 1], nrsem.at[e - 1], dev(dx=e)))
    for c in arrivals:
        c.wait_recv()
    numerator = part[pl.ds(0, ROWS), :]
    for e in range(3):
        numerator = numerator + partr[e].astype(F32)
    root_mean = jnp.sqrt(jnp.mean(numerator * numerator, axis=-1, keepdims=True) + EPSILON)
    normed = numerator / root_mean
    grad = gbuf[...].astype(F32)
    ngall[0] = ((grad - normed * jnp.mean(grad * normed, axis=-1, keepdims=True)) / root_mean).astype(BF)
    from_x = [
        send(ngall.at[0], ngall.at[4 - e], gsem.at[e - 1], grsem.at[e - 1], dev(dx=e)) for e in (2, 1, 3)
    ]
    att_ref[...] = normed.astype(BF)
    for c in from_x:
        c.wait_recv()

    queries = qall[...].reshape(4 * ROWS, D)
    grads = ngall[...].reshape(4 * ROWS, D)
    dqacc[...] = jnp.zeros_like(dqacc)
    from_y = {}
    for d in BACK:
        keys = kv[d, :, 0].reshape(2 * ROWS, D)
        values = kv[d, :, 1].reshape(2 * ROWS, D)
        coefficient = (2.0 * s_ref[d] * dot_last(grads, values)).astype(BF)
        dkvs[d, :, 0] = dot_first(coefficient, queries).astype(BF).reshape(2, ROWS, D)
        dkvs[d, :, 1] = dot_first(w_ref[d], grads).astype(BF).reshape(2, ROWS, D)
        from_y[d] = []
        for r in (0, 1):
            for f in range(4):
                if (r, f) != (0, 0):
                    rows = pl.ds(pl.multiple_of(((y + f) % 4) * 32, 32), 32)
                    from_y[d].append(
                        send(
                            dkvs.at[d, r, :, rows, :], yr.at[d, r * 4 + f],
                            ysem.at[d, r * 4 + f], yrsem.at[d, r * 4 + f], dev(dcore=r, dy=f),
                        )
                    )
        dqacc[...] += dot(coefficient, keys)
    arrivals = []
    for e in (1, 2, 3):
        dqs[e - 1] = dqacc[pl.ds(e * ROWS, ROWS), :].astype(BF)
        arrivals.append(send(dqs.at[e - 1], dqr.at[e - 1], dsem.at[e - 1], drsem.at[e - 1], dev(dx=e)))

    from_z = []
    for d in BACK:
        for c in from_y[d]:
            c.wait_recv()
        total = dkvs[d, 0, :, mine, :].astype(F32)
        for i in range(1, 8):
            total = total + yr[d, i].astype(F32)
        zs[d] = total.astype(BF).reshape(4, 16, D)
        for m in range(4):
            if (d, m) != (0, 0):
                from_z.append(
                    send(
                        zs.at[d, (zlo + m) % 4], zr.at[d * 4 + m],
                        asem.at[d * 4 + m], arsem.at[d * 4 + m], dev(dzhi=4 - d, dzlo=m),
                    )
                )
    for c in arrivals:
        c.wait_recv()
    query_grad = dqacc[pl.ds(0, ROWS), :]
    for e in range(3):
        query_grad = query_grad + dqr[e].astype(F32)
    dq_ref[...] = query_grad.astype(BF)
    for c in from_z:
        c.wait_recv()
    total = zs[0, zlo].astype(F32)
    for i in range(1, 16):
        total = total + zr[i].astype(F32)
    place = pl.ds(pl.multiple_of(y * 32 + (zlo % 2) * 16, 16), 16)
    fin[...] = total.astype(BF)
    dkv_ref[zlo // 2, place, :] = total.astype(BF)
    last = []
    for f in range(4):
        for m in range(4):
            if (f, m) != (0, 0):
                last.append(
                    send(
                        fin, dkv_ref.at[zlo // 2, place, :],
                        osem.at[f * 4 + m], orsem.at[f * 4 + m], dev(dy=f, dzlo=m),
                    )
                )
    for c in last:
        c.wait_recv()
    for c in sent:
        c.wait_send()


def local(query_rows, key_rows, value_rows, out_grad):
    dma = pltpu.SemaphoreType.DMA
    vmem = pl.BlockSpec(memory_space=pltpu.VMEM)
    attended, query_grad, kv_grad = pl.pallas_call(
        kernel,
        out_shape=(
            jax.ShapeDtypeStruct((ROWS, D), BF),
            jax.ShapeDtypeStruct((ROWS, D), BF),
            jax.ShapeDtypeStruct((2, ROWS, D), BF),
        ),
        in_specs=[pl.BlockSpec(memory_space=pl.ANY)] * 4,
        out_specs=(vmem, vmem, vmem),
        scratch_shapes=[
            pltpu.VMEM((4, ROWS, D), BF),
            pltpu.VMEM((4, ROWS, D), BF),
            pltpu.VMEM((ROWS, D), BF),
            pltpu.VMEM((4, 2, 2, ROWS, D), BF),
            pltpu.VMEM((4, 4 * ROWS, 2 * ROWS), F32),
            pltpu.VMEM((4, 4 * ROWS, 2 * ROWS), BF),
            pltpu.VMEM((4 * ROWS, D), F32),
            pltpu.VMEM((3, ROWS, D), BF),
            pltpu.VMEM((3, ROWS, D), BF),
            pltpu.VMEM((4 * ROWS, D), F32),
            pltpu.VMEM((3, ROWS, D), BF),
            pltpu.VMEM((3, ROWS, D), BF),
            pltpu.VMEM((4, 2, 2, ROWS, D), BF),
            pltpu.VMEM((4, 8, 2, 32, D), BF),
            pltpu.VMEM((4, 4, 16, D), BF),
            pltpu.VMEM((16, 16, D), BF),
            pltpu.VMEM((16, D), BF),
            dma((4,)), dma((3,)), dma((3,)), dma((2,)), dma((3,)), dma((3,)), dma((3, 8)), dma((3, 8)),
            dma((3,)), dma((3,)), dma((3,)), dma((3,)), dma((3,)), dma((3,)),
            dma((4, 8)), dma((4, 8)), dma((16,)), dma((16,)), dma((16,)), dma((16,)),
        ],
        compiler_params=pltpu.CompilerParams(
            collective_id=0, has_side_effects=True, vmem_limit_bytes=48 * 2**20
        ),
    )(query_rows, key_rows, value_rows, out_grad)
    return attended, query_grad, kv_grad[0], kv_grad[1]


def solution(mesh):
    return jax.shard_map(
        local,
        mesh=mesh,
        in_specs=(P("seq", "head"), P("seq", None), P("seq", None), P("seq", "head")),
        out_specs=(P("seq", "head"), P("seq", "head"), P("seq", None), P("seq", None)),
        check_vma=False,
    )
```

time: 479 us -> 61.7 us (0.13); the launches traced: 473 us -> 61.3 us
  waiting for transfers between devices: 194 us -> 0 us
  matrix products: 100 us -> 0 us
  Pallas kernels: 0 us -> 55.8 us
  blocking collectives: 44.3 us -> 0 us
  local copies, waits for them, and re-layouts: 45.7 us -> 4.88 us
  other arithmetic: 39.2 us -> 0 us
  starting transfers between devices: 23.3 us -> 0 us
  between operations: 14.2 us -> 0.65 us
  loops' own time: 12 us -> 0 us
    dot_general x125 -> x0, matrix products: 100 us -> none  [the longest x34 20.8 us: columns(): jnp.dot(source, picker(picked, source.shape[-1]), preferred_element_type=...]
    all_gather x2 -> x0, waiting for transfers between devices: 87.8 us -> none  [carried_in(): pieces = lax.all_gather(running, axis)]
    psum x1 -> x0, waiting for transfers between devices: 79 us -> none  [local(): lax.psum(key_part.astype(jnp.bfloat16), 'head').astype(jnp.float32)]
    pallas_call x0 -> x1, Pallas kernels: none -> 55.8 us  [local(): pl.pallas_call(kernel, out_shape=(jax.ShapeDtypeStruct((ROWS, D), BF), ja...]
    all_gather x4 -> x0, blocking collectives: 44.3 us -> none  [the longest x3 42.1 us: entering(): pieces = lax.all_gather(running.astype(jnp.bfloat16), axis)]
    dynamic_slice x50 -> x0, local copies, waits for them, and re-layouts: 35.7 us -> none  [the longest x16 12.5 us: add_query_grad(): lax.dynamic_slice_in_dim(first_all, start_feature, sub_block.shape[0])]
    select_n x48 -> x0, other arithmetic: 33.6 us -> none  [multiplicity(): return jnp.where(first_index == second_index, 1.0, 2.0).astype(jnp.float32)]
    all_to_all x4 -> x0, waiting for transfers between devices: 27.5 us -> none  [the longest x1 15.4 us: sum_at_owner(): lax.all_to_all(pieces, axis, split_axis=0, concat_axis=0, tiled=True)]
  transfers between devices with their start and end apart: 7 -> 0, of which waited for: 5 -> 0; matrix products, arithmetic and copies ran while one was open for 30% -> 0% of each run, Pallas kernels for 0% -> 0%
where the time goes in v1:
time: 61.7 us; the launch traced here: 61.3 us
  Pallas kernels  55.8 us (90%)
  local copies, waits for them, and re-layouts  4.88 us (8%)
  between operations  0.65 us (1%)
    pallas_call x1, Pallas kernels, local(): pl.pallas_call(kernel, out_shape=(jax.ShapeDtypeStruct((ROWS, D), BF), ja...  55.8 us
    unnamed x10, local copies, waits for them, and re-layouts  4.25 us

profile of v1, /device:TPU:6, one launch (start us, length us, event | category | flops | bytes accessed | tf_op | source)
XLA Modules:
  0.0 61.3 jit_solution(4341091605397789743)
XLA Ops:
  0.6 0.0 copy-start
  0.6 0.7 %copy-done = bf16[128,128]{1,0:T(8,128)(2,1)S(1)} copy-done((bf16[128,128]{1,0:T(8,128)(2,1)S(1)}, bf16[128,128]{1,0:T(8,128)(2,1)}, u32[]{:S(2)}) %copy-start) | copy-done | bytes 32792
  1.4 0.0 copy-start.1
  1.4 0.8 %copy-done.1 = bf16[128,128]{1,0:T(8,128)(2,1)S(1)} copy-done((bf16[128,128]{1,0:T(8,128)(2,1)S(1)}, bf16[128,128]{1,0:T(8,128)(2,1)}, u32[]{:S(2)}) %copy-start.1) | copy-done | bytes 32792
  2.1 0.0 copy-start.2
  2.2 0.8 %copy-done.2 = bf16[128,128]{1,0:T(8,128)(2,1)S(1)} copy-done((bf16[128,128]{1,0:T(8,128)(2,1)S(1)}, bf16[128,128]{1,0:T(8,128)(2,1)}, u32[]{:S(2)}) %copy-start.2) | copy-done | bytes 32792
  2.9 0.0 copy-start.3
  2.9 0.8 %copy-done.3 = bf16[128,128]{1,0:T(8,128)(2,1)S(1)} copy-done((bf16[128,128]{1,0:T(8,128)(2,1)S(1)}, bf16[128,128]{1,0:T(8,128)(2,1)}, u32[]{:S(2)}) %copy-start.3) | copy-done | bytes 32792
  3.7 55.8 %shard_map.75 = (bf16[128,128]{1,0:T(8,128)(2,1)S(1)}, bf16[128,128]{1,0:T(8,128)(2,1)S(1)}, bf16[2,128,128]{2,1,0:T(8,128)(2,1)S(1)}) custom-call(bf16[128,128]{1,0:T(8,128)(2,1)S(1)} %copy-done, bf16[128,128]{1,0:T(8,128)(2,1)S(1)} %copy-done.1, bf16[128,128]{1,0:T(8,128)(2,1)S(1)} %copy-done.2, bf16[128,128]{1,0:T(8,128)(2,1)S(1)} %copy-done.3), custom_call_target="tpu_custom_call" | custom-call | tf_op jit(solution)/shard_map/pallas_call | solution.py:225
  59.5 0.6 %slice_bitcast_fusion = (bf16[128,128]{1,0:T(8,128)(2,1)}, bf16[128,128]{1,0:T(8,128)(2,1)}) fusion(bf16[2,128,128]{2,1,0:T(8,128)(2,1)S(1)} %get-tuple-element.9), kind=kLoop, calls=%fused_computation | loop fusion | bytes 131072 | tf_op jit(solution)/shard_map/squeeze | solution.py:260
  60.1 0.6 %copy.10 = bf16[128,128]{1,0:T(8,128)(2,1)} copy(bf16[128,128]{1,0:T(8,128)(2,1)S(1)} %get-tuple-element.16) | data formatting | bytes 65536
  60.7 0.6 %copy.11 = bf16[128,128]{1,0:T(8,128)(2,1)} copy(bf16[128,128]{1,0:T(8,128)(2,1)S(1)} %get-tuple-element.17) | data formatting | bytes 65536
Async XLA Ops:
  0.6 0.8 %copy-start = (bf16[128,128]{1,0:T(8,128)(2,1)S(1)}, bf16[128,128]{1,0:T(8,128)(2,1)}, u32[]{:S(2)}) copy-start(bf16[128,128]{1,0:T(8,128)(2,1)} %q_in.1) | copy-start | bytes 98308
  1.4 0.8 %copy-start.1 = (bf16[128,128]{1,0:T(8,128)(2,1)S(1)}, bf16[128,128]{1,0:T(8,128)(2,1)}, u32[]{:S(2)}) copy-start(bf16[128,128]{1,0:T(8,128)(2,1)} %k_in.1) | copy-start | bytes 98308
  2.1 0.8 %copy-start.2 = (bf16[128,128]{1,0:T(8,128)(2,1)S(1)}, bf16[128,128]{1,0:T(8,128)(2,1)}, u32[]{:S(2)}) copy-start(bf16[128,128]{1,0:T(8,128)(2,1)} %v_in.1) | copy-start | bytes 98308
  2.9 0.8 %copy-start.3 = (bf16[128,128]{1,0:T(8,128)(2,1)S(1)}, bf16[128,128]{1,0:T(8,128)(2,1)}, u32[]{:S(2)}) copy-start(bf16[128,128]{1,0:T(8,128)(2,1)} %g_in.1) | copy-start | bytes 98308

commit v2 on v1

v2 whole, which is shorter than its diff:
```python
import jax
import jax.numpy as jnp
from jax import lax
from jax.experimental import pallas as pl
from jax.experimental.pallas import tpu as pltpu
from jax.sharding import PartitionSpec as P

MESH = pl.DeviceIdType.MESH
EPSILON = 1e-06
BF = jnp.bfloat16
F32 = jnp.float32
ROWS = 128
D = 128
BACK = (2, 1, 3, 0)


def dot_last(a, b):
    return lax.dot_general(a, b, (((1,), (1,)), ((), ())), preferred_element_type=F32)


def dot_first(a, b):
    return lax.dot_general(a, b, (((0,), (0,)), ((), ())), preferred_element_type=F32)


def dot(a, b):
    return jnp.dot(a, b, preferred_element_type=F32)


def kernel(
    in_ref,
    out_ref,
    qall, ngall, gbuf, kv, s_ref, w_ref, part, parts, partr,
    dqacc, dqs, dqr, dkvs, cr, ys, yr, zs, zr, fin,
    lsem, zsem, zrsem, csem, qsem, qrsem, fsem, frsem, psem, prsem,
    nsem, nrsem, gsem, grsem, dsem, drsem, ysem, yrsem, asem, arsem, osem, orsem,
):
    seq, head = lax.axis_index("seq"), lax.axis_index("head")
    zhi, x, core = seq // 8, (seq // 2) % 4, seq % 2
    zlo, y = head // 4, head % 4

    def dev(dzhi=0, dx=0, dcore=0, dzlo=0, dy=0):
        return (
            (((zhi + dzhi) % 4) * 4 + (x + dx) % 4) * 2 + (core + dcore) % 2,
            ((zlo + dzlo) % 4) * 4 + (y + dy) % 4,
        )

    has = {d: zhi >= d for d in range(4)}
    feeds = {d: zhi + d <= 3 for d in range(4)}

    peers = [dev(dzhi=d, dzlo=m) for d in (2, 1, 3, 0) for m in range(4) if (d, m) != (0, 0)]
    peers += [dev(dy=f, dzlo=m) for f in (1, 2, 3) for m in (1, 2, 3)]
    peers += [dev(dx=e) for e in (1, 2, 3)]
    peers += [dev(dy=f) for f in (1, 2, 3)] + [dev(dcore=1)]
    zr[...] = jnp.zeros_like(zr)
    barrier = pltpu.get_barrier_semaphore()
    for p in peers:
        pl.semaphore_signal(barrier, 1, device_id=p, device_id_type=MESH)
    loads = [
        pltpu.make_async_copy(in_ref.at[1], kv.at[0, 0, 0], lsem.at[0]),
        pltpu.make_async_copy(in_ref.at[2], kv.at[0, 0, 1], lsem.at[1]),
        pltpu.make_async_copy(in_ref.at[0], qall.at[0], lsem.at[2]),
        pltpu.make_async_copy(in_ref.at[3], gbuf, lsem.at[3]),
    ]
    for c in loads:
        c.start()
    for c in loads:
        c.wait()
    pl.semaphore_wait(barrier, len(peers))

    sent = []

    def make(src, dst, ssem, rsem, to, only=None):
        c = pltpu.make_async_remote_copy(
            src_ref=src, dst_ref=dst, send_sem=ssem, recv_sem=rsem, device_id=to, device_id_type=MESH
        )
        sent.append((c, only))
        return c

    def started(c):
        c.start()
        return c

    mine = pl.ds(pl.multiple_of(y * 32, 32), 32)
    from_z = {}
    for d in (1, 2, 3):
        from_z[d] = [
            make(
                kv.at[0, 0, :, mine, :], kv.at[d, 0, :, mine, :],
                zsem.at[d - 1], zrsem.at[d - 1], dev(dzhi=d), feeds[d],
            )
        ]
    for d in (2, 3, 1):

        @pl.when(feeds[d])
        def _():
            for c in from_z[d]:
                c.start()

    from_core = started(make(kv.at[0, 0], kv.at[0, 1], csem.at[0], csem.at[1], dev(dcore=1)))
    from_x = [
        started(make(qall.at[0], qall.at[4 - e], qsem.at[e - 1], qrsem.at[e - 1], dev(dx=e)))
        for e in (2, 1, 3)
    ]

    gap = lax.broadcasted_iota(jnp.int32, (ROWS, ROWS), 1) - lax.broadcasted_iota(
        jnp.int32, (ROWS, ROWS), 0
    )

    def forward(d):
        queries = qall[...].reshape(4 * ROWS, D)
        keys = kv[d, :, 0].reshape(2 * ROWS, D)
        values = kv[d, :, 1].reshape(2 * ROWS, D)
        products = dot_last(queries, keys)
        for e in range(4):
            block = (zhi * 4 + (x + e) % 4) * 2 + core
            for r in range(2):
                other = (((zhi + 4 - d) % 4) * 4 + x) * 2 + (core + r) % 2
                tile = products[e * ROWS : (e + 1) * ROWS, r * ROWS : (r + 1) * ROWS]
                if d == 0:
                    tile = jnp.where(gap <= (block - other) * ROWS, tile, 0.0)
                s_ref[d, pl.ds(e * ROWS, ROWS), pl.ds(r * ROWS, ROWS)] = tile
                w_ref[d, pl.ds(e * ROWS, ROWS), pl.ds(r * ROWS, ROWS)] = (tile * tile).astype(BF)
        return dot(w_ref[d], values)

    passed, from_y = {}, {}
    for d in (1, 2, 3):
        passed[d] = make(
            kv.at[d, 0], kv.at[d, 1], psem.at[d - 1], prsem.at[d - 1], dev(dcore=1), has[d]
        )
    for d in (1, 2, 3):
        from_y[d] = [
            make(
                kv.at[d, 0, :, mine, :], kv.at[d, 0, :, mine, :],
                fsem.at[d - 1, f], frsem.at[d - 1, f], dev(dy=f), has[d],
            )
            for f in (2, 1, 3)
        ]

    from_core.wait_recv()
    for c in from_x:
        c.wait_recv()
    part[...] = forward(0)
    for d in (1, 3, 2):

        @pl.when(has[d])
        def _():
            from_z[d][0].wait_recv()
            for c in from_y[d]:
                c.start()

    def hand_on(d, arriving):
        @pl.when(has[d])
        def _():
            for c in arriving:
                c.wait_recv()
            passed[d].start()

    def use(d):
        @pl.when(has[d])
        def _():
            passed[d].wait_recv()
            part[...] += forward(d)

    hand_on(1, from_y[1])
    hand_on(3, from_y[3])
    use(1)
    hand_on(2, from_y[2])
    use(3)
    use(2)

    arrivals = []
    for e in (2, 1, 3):
        parts[e - 1] = part[pl.ds(e * ROWS, ROWS), :].astype(BF)
        arrivals.append(
            started(make(parts.at[e - 1], partr.at[e - 1], nsem.at[e - 1], nrsem.at[e - 1], dev(dx=e)))
        )
    for c in arrivals:
        c.wait_recv()
    numerator = part[pl.ds(0, ROWS), :]
    for e in range(3):
        numerator = numerator + partr[e].astype(F32)
    root_mean = jnp.sqrt(jnp.mean(numerator * numerator, axis=-1, keepdims=True) + EPSILON)
    normed = numerator / root_mean
    grad = gbuf[...].astype(F32)
    ngall[0] = ((grad - normed * jnp.mean(grad * normed, axis=-1, keepdims=True)) / root_mean).astype(BF)
    from_x = [
        started(make(ngall.at[0], ngall.at[4 - e], gsem.at[e - 1], grsem.at[e - 1], dev(dx=e)))
        for e in (2, 1, 3)
    ]
    out_ref[0] = normed.astype(BF)
    for c in from_x:
        c.wait_recv()

    passed, from_y = {}, {}
    for d in range(4):
        passed[d] = make(dkvs.at[d, 1], cr.at[d], ysem.at[d, 0], yrsem.at[d, 0], dev(dcore=1), has[d])
        from_y[d] = []
        for f in (2, 1, 3):
            rows = pl.ds(pl.multiple_of(((y + f) % 4) * 32, 32), 32)
            from_y[d].append(
                make(ys.at[d, :, rows, :], yr.at[d, f], ysem.at[d, f], yrsem.at[d, f], dev(dy=f), has[d])
            )

    def backward(d):
        @pl.when(has[d])
        def _():
            queries = qall[...].reshape(4 * ROWS, D)
            grads = ngall[...].reshape(4 * ROWS, D)
            keys = kv[d, :, 0].reshape(2 * ROWS, D)
            values = kv[d, :, 1].reshape(2 * ROWS, D)
            coefficient = (2.0 * s_ref[d] * dot_last(grads, values)).astype(BF)
            dkvs[d, :, 0] = dot_first(coefficient, queries).astype(BF).reshape(2, ROWS, D)
            dkvs[d, :, 1] = dot_first(w_ref[d], grads).astype(BF).reshape(2, ROWS, D)
            passed[d].start()
            dqacc[...] += dot(coefficient, keys)

    def over_y(d):
        @pl.when(has[d])
        def _():
            passed[d].wait_recv()
            ys[d] = (dkvs[d, 0].astype(F32) + cr[d].astype(F32)).astype(BF)
            for c in from_y[d]:
                c.start()

    dqacc[...] = jnp.zeros_like(dqacc)
    late = []
    for d in BACK:
        backward(d)
        late.append(d)
        if len(late) > 2:
            over_y(late.pop(0))
    for d in late:
        over_y(d)
    arrivals = []
    for e in (2, 1, 3):
        dqs[e - 1] = dqacc[pl.ds(e * ROWS, ROWS), :].astype(BF)
        arrivals.append(
            started(make(dqs.at[e - 1], dqr.at[e - 1], dsem.at[e - 1], drsem.at[e - 1], dev(dx=e)))
        )

    from_z = {}
    for d in BACK:
        from_z[d] = []
        for m in (3, 2, 1, 0):
            if (d, m) != (0, 0):
                from_z[d].append(
                    make(
                        zs.at[d, (zlo + m) % 4], zr.at[d * 4 + m],
                        asem.at[d * 4 + m], arsem.at[d * 4 + m], dev(dzhi=4 - d, dzlo=m), has[d],
                    )
                )

        @pl.when(has[d])
        def _():
            for c in from_y[d]:
                c.wait_recv()
            total = ys[d, :, mine, :].astype(F32)
            for i in range(1, 4):
                total = total + yr[d, i].astype(F32)
            zs[d] = total.astype(BF).reshape(4, 16, D)
            for c in from_z[d]:
                c.start()

    for c in arrivals:
        c.wait_recv()
    query_grad = dqacc[pl.ds(0, ROWS), :]
    for e in range(3):
        query_grad = query_grad + dqr[e].astype(F32)
    out_ref[1] = query_grad.astype(BF)
    for d in (0, 1, 3, 2):

        @pl.when(feeds[d])
        def _():
            for c in from_z[d]:
                c.wait_recv()

    total = zs[0, zlo].astype(F32)
    for i in range(1, 16):
        total = total + zr[i].astype(F32)
    place = pl.ds(pl.multiple_of(y * 32 + (zlo % 2) * 16, 16), 16)
    fin[...] = total.astype(BF)
    out_ref[2 + zlo // 2, place, :] = total.astype(BF)
    last = []
    for f in (2, 1, 3, 0):
        for m in (3, 2, 1, 0):
            if (f, m) != (0, 0):
                last.append(
                    started(
                        make(
                            fin, out_ref.at[2 + zlo // 2, place, :],
                            osem.at[f * 4 + m], orsem.at[f * 4 + m], dev(dy=f, dzlo=m),
                        )
                    )
                )
    for c in last:
        c.wait_recv()
    for c, only in sent:
        if only is None:
            c.wait_send()
    for only in (*feeds.values(), *has.values()):

        @pl.when(only)
        def _():
            for c, o in sent:
                if o is only:
                    c.wait_send()


def local(query_rows, key_rows, value_rows, out_grad):
    dma = pltpu.SemaphoreType.DMA
    packed = pl.pallas_call(
        kernel,
        out_shape=jax.ShapeDtypeStruct((4, ROWS, D), BF),
        in_specs=[pl.BlockSpec(memory_space=pltpu.VMEM)],
        out_specs=pl.BlockSpec(memory_space=pltpu.VMEM),
        scratch_shapes=[
            pltpu.VMEM((4, ROWS, D), BF),
            pltpu.VMEM((4, ROWS, D), BF),
            pltpu.VMEM((ROWS, D), BF),
            pltpu.VMEM((4, 2, 2, ROWS, D), BF),
            pltpu.VMEM((4, 4 * ROWS, 2 * ROWS), F32),
            pltpu.VMEM((4, 4 * ROWS, 2 * ROWS), BF),
            pltpu.VMEM((4 * ROWS, D), F32),
            pltpu.VMEM((3, ROWS, D), BF),
            pltpu.VMEM((3, ROWS, D), BF),
            pltpu.VMEM((4 * ROWS, D), F32),
            pltpu.VMEM((3, ROWS, D), BF),
            pltpu.VMEM((3, ROWS, D), BF),
            pltpu.VMEM((4, 2, 2, ROWS, D), BF),
            pltpu.VMEM((4, 2, ROWS, D), BF),
            pltpu.VMEM((4, 2, ROWS, D), BF),
            pltpu.VMEM((4, 4, 2, 32, D), BF),
            pltpu.VMEM((4, 4, 16, D), BF),
            pltpu.VMEM((16, 16, D), BF),
            pltpu.VMEM((16, D), BF),
            dma((4,)), dma((3,)), dma((3,)), dma((2,)), dma((3,)), dma((3,)), dma((3, 4)), dma((3, 4)), dma((3,)), dma((3,)),
            dma((3,)), dma((3,)), dma((3,)), dma((3,)), dma((3,)), dma((3,)),
            dma((4, 4)), dma((4, 4)), dma((16,)), dma((16,)), dma((16,)), dma((16,)),
        ],
        compiler_params=pltpu.CompilerParams(
            collective_id=0, has_side_effects=True, vmem_limit_bytes=48 * 2**20
        ),
    )(jnp.stack((query_rows, key_rows, value_rows, out_grad)))
    return packed[0], packed[1], packed[2], packed[3]


def solution(mesh):
    return jax.shard_map(
        local,
        mesh=mesh,
        in_specs=(P("seq", "head"), P("seq", None), P("seq", None), P("seq", "head")),
        out_specs=(P("seq", "head"), P("seq", "head"), P("seq", None), P("seq", None)),
        check_vma=False,
    )
```

time: 61.7 us -> 57.3 us (0.929)
  local copies, waits for them, and re-layouts: 4.88 us -> 0.65 us
  Pallas kernels: 55.8 us -> 54.6 us
  other arithmetic: 0 us -> 0.83 us
    unnamed x10 -> x0, local copies, waits for them, and re-layouts: 4.25 us -> none
    pallas_call x1, Pallas kernels: 55.8 us -> 54.6 us  [local(): pl.pallas_call(kernel, out_shape=jax.ShapeDtypeStruct((4, ROWS, D), BF),...]
    another operation x0 -> x1, other arithmetic: none -> 0.83 us  [local(): jnp.stack((query_rows, key_rows, value_rows, out_grad))]
where the time goes in v2:
time: 57.3 us; the launch traced here: 56.7 us
  Pallas kernels  54.6 us (95%)
  other arithmetic  0.83 us (1%)
  local copies, waits for them, and re-layouts  0.65 us (1%)
  between operations  0.64 us (1%)
    pallas_call x1, Pallas kernels, local(): pl.pallas_call(kernel, out_shape=jax.ShapeDtypeStruct((4, ROWS, D), BF),...  54.6 us

profile of v2, /device:TPU:6, one launch (start us, length us, event | category | flops | bytes accessed | tf_op | source)
XLA Modules:
  0.0 56.7 jit_solution(7827985239689417120)
XLA Ops:
  0.6 0.8 %pad_maximum_fusion.in_ref = bf16[4,128,128]{2,1,0:T(8,128)(2,1)S(1)} fusion(bf16[1,128,128]{2,1,0:T(8,128)(2,1)} %bitcast.12, bf16[1,128,128]{2,1,0:T(8,128)(2,1)} %bitcast.13, bf16[1,128,128]{2,1,0:T(8,128)(2,1)} %bitcast.14, bf16[1,128,128]{2,1,0:T(8,128)(2,1)} %bitcast.15), kind=kLoop, calls=%fused_computation | loop fusion | flops 196608 | bytes 262144 | tf_op jit(solution)/shard_map/stack | solution.py:343
  1.5 54.6 %shard_map.75 = bf16[4,128,128]{2,1,0:T(8,128)(2,1)S(1)} custom-call(bf16[4,128,128]{2,1,0:T(8,128)(2,1)S(1)} %pad_maximum_fusion.in_ref), custom_call_target="tpu_custom_call" | custom-call | tf_op jit(solution)/shard_map/pallas_call | solution.py:311
  56.1 0.7 %slice_bitcast_fusion = (bf16[128,128]{1,0:T(8,128)(2,1)}, bf16[128,128]{1,0:T(8,128)(2,1)}, bf16[128,128]{1,0:T(8,128)(2,1)}, bf16[128,128]{1,0:T(8,128)(2,1)}) fusion(bf16[4,128,128]{2,1,0:T(8,128)(2,1)S(1)} %shard_map.75), kind=kLoop, calls=%fused_computation.1 | loop fusion | bytes 262144 | tf_op jit(solution)/shard_map/squeeze | solution.py:344

commit v3 on v2

--- a/solution.py
+++ b/solution.py
@@ -1,3 +1,5 @@
+import functools
+
 import jax
 import jax.numpy as jnp
 from jax import lax
@@ -11,7 +13,7 @@
 F32 = jnp.float32
 ROWS = 128
 D = 128
-BACK = (2, 1, 3, 0)
+BACK = (2, 3, 1, 0)
 
 
 def dot_last(a, b):
@@ -47,13 +49,27 @@
     has = {d: zhi >= d for d in range(4)}
     feeds = {d: zhi + d <= 3 for d in range(4)}
 
-    peers = [dev(dzhi=d, dzlo=m) for d in (2, 1, 3, 0) for m in range(4) if (d, m) != (0, 0)]
-    peers += [dev(dy=f, dzlo=m) for f in (1, 2, 3) for m in (1, 2, 3)]
-    peers += [dev(dx=e) for e in (1, 2, 3)]
-    peers += [dev(dy=f) for f in (1, 2, 3)] + [dev(dcore=1)]
+    near = [dev(dzlo=m) for m in (1, 2, 3)]
+    near += [dev(dy=f, dzlo=m) for f in (1, 2, 3) for m in (1, 2, 3)]
+    near += [dev(dx=e) for e in (1, 2, 3)]
+    near += [dev(dcore=r, dy=f) for r in (0, 1) for f in range(4) if (r, f) != (0, 0)]
     zr[...] = jnp.zeros_like(zr)
     barrier = pltpu.get_barrier_semaphore()
-    for p in peers:
+    owner = zlo < 2
+    for d in (2, 3, 1):
+
+        @pl.when(has[d])
+        def _():
+            pl.semaphore_signal(barrier, 1, device_id=dev(dzhi=4 - d), device_id_type=MESH)
+
+    for d in (1, 2, 3):
+
+        @pl.when(jnp.logical_and(feeds[d], owner))
+        def _():
+            for m in range(4):
+                pl.semaphore_signal(barrier, 1, device_id=dev(dzhi=d, dzlo=m), device_id_type=MESH)
+
+    for p in near:
         pl.semaphore_signal(barrier, 1, device_id=p, device_id_type=MESH)
     loads = [
         pltpu.make_async_copy(in_ref.at[1], kv.at[0, 0, 0], lsem.at[0]),
@@ -65,7 +81,7 @@
         c.start()
     for c in loads:
         c.wait()
-    pl.semaphore_wait(barrier, len(peers))
+    pl.semaphore_wait(barrier, len(near) + (3 - zhi) + 2 * zhi)
 
     sent = []
 
@@ -123,9 +139,9 @@
         return dot(w_ref[d], values)
 
     passed, from_y = {}, {}
-    for d in (1, 2, 3):
+    for d in (1, 3):
         passed[d] = make(
-            kv.at[d, 0], kv.at[d, 1], psem.at[d - 1], prsem.at[d - 1], dev(dcore=1), has[d]
+            kv.at[d, 0], kv.at[d, 1], csem.at[d + 1], csem.at[d + 2], dev(dcore=1), has[d]
         )
     for d in (1, 2, 3):
         from_y[d] = [
@@ -135,6 +151,13 @@
             )
             for f in (2, 1, 3)
         ]
+    for f in (2, 1, 3, 0):
+        from_y[2].append(
+            make(
+                kv.at[2, 0, :, mine, :], kv.at[2, 1, :, mine, :],
+                psem.at[f], prsem.at[f], dev(dcore=1, dy=f), has[2],
+            )
+        )
 
     from_core.wait_recv()
     for c in from_x:
@@ -164,9 +187,14 @@
     hand_on(1, from_y[1])
     hand_on(3, from_y[3])
     use(1)
-    hand_on(2, from_y[2])
     use(3)
-    use(2)
+
+    @pl.when(has[2])
+    def _():
+        for c in from_y[2]:
+            c.wait_recv()
+        part[...] += forward(2)
+
 
     arrivals = []
     for e in (2, 1, 3):
@@ -193,8 +221,20 @@
 
     passed, from_y = {}, {}
     for d in range(4):
+        from_y[d] = []
+        if d == 2:
+            for r in (0, 1):
+                for f in (2, 1, 3, 0):
+                    if (r, f) != (0, 0):
+                        rows = pl.ds(pl.multiple_of(((y + f) % 4) * 32, 32), 32)
+                        from_y[d].append(
+                            make(
+                                dkvs.at[d, r, :, rows, :], yr.at[d + 2 * r, f],
+                                ysem.at[d + 2 * r, f], yrsem.at[d + 2 * r, f], dev(dcore=r, dy=f), has[d],
+                            )
+                        )
+            continue
         passed[d] = make(dkvs.at[d, 1], cr.at[d], ysem.at[d, 0], yrsem.at[d, 0], dev(dcore=1), has[d])
-        from_y[d] = []
         for f in (2, 1, 3):
             rows = pl.ds(pl.multiple_of(((y + f) % 4) * 32, 32), 32)
             from_y[d].append(
@@ -211,7 +251,8 @@
             coefficient = (2.0 * s_ref[d] * dot_last(grads, values)).astype(BF)
             dkvs[d, :, 0] = dot_first(coefficient, queries).astype(BF).reshape(2, ROWS, D)
             dkvs[d, :, 1] = dot_first(w_ref[d], grads).astype(BF).reshape(2, ROWS, D)
-            passed[d].start()
+            for c in from_y[2] if d == 2 else (passed[d],):
+                c.start()
             dqacc[...] += dot(coefficient, keys)
 
     def over_y(d):
@@ -226,7 +267,8 @@
     late = []
     for d in BACK:
         backward(d)
-        late.append(d)
+        if d != 2:
+            late.append(d)
         if len(late) > 2:
             over_y(late.pop(0))
     for d in late:
@@ -238,28 +280,34 @@
             started(make(dqs.at[e - 1], dqr.at[e - 1], dsem.at[e - 1], drsem.at[e - 1], dev(dx=e)))
         )
 
-    from_z = {}
+    to_z = {}
+    other = {o: zlo != o for o in (0, 1)}
     for d in BACK:
-        from_z[d] = []
-        for m in (3, 2, 1, 0):
-            if (d, m) != (0, 0):
-                from_z[d].append(
-                    make(
-                        zs.at[d, (zlo + m) % 4], zr.at[d * 4 + m],
-                        asem.at[d * 4 + m], arsem.at[d * 4 + m], dev(dzhi=4 - d, dzlo=m), has[d],
-                    )
-                )
+        to_z[d] = []
+        for o in (0, 1):
+            only = has[d] if d else other[o]
+            c = make(
+                zs.at[d, o], zr.at[d * 4 + zlo], asem.at[d * 2 + o], arsem.at[d * 4 + zlo],
+                dev(dzhi=4 - d, dzlo=o + 4 - zlo), only,
+            )
+            to_z[d].append((c, only))
 
         @pl.when(has[d])
         def _():
             for c in from_y[d]:
                 c.wait_recv()
-            total = ys[d, :, mine, :].astype(F32)
+            total = (dkvs[d, 0, :, mine, :] if d == 2 else ys[d, :, mine, :]).astype(F32)
             for i in range(1, 4):
                 total = total + yr[d, i].astype(F32)
-            zs[d] = total.astype(BF).reshape(4, 16, D)
-            for c in from_z[d]:
-                c.start()
+            if d == 2:
+                for i in range(4):
+                    total = total + yr[4, i].astype(F32)
+            zs[d] = total.astype(BF)
+            for c, only in to_z[d]:
+                if d:
+                    c.start()
+                else:
+                    pl.when(only)(c.start)
 
     for c in arrivals:
         c.wait_recv()
@@ -267,43 +315,73 @@
     for e in range(3):
         query_grad = query_grad + dqr[e].astype(F32)
     out_ref[1] = query_grad.astype(BF)
-    for d in (0, 1, 3, 2):
-
-        @pl.when(feeds[d])
-        def _():
-            for c in from_z[d]:
-                c.wait_recv()
-
-    total = zs[0, zlo].astype(F32)
-    for i in range(1, 16):
-        total = total + zr[i].astype(F32)
-    place = pl.ds(pl.multiple_of(y * 32 + (zlo % 2) * 16, 16), 16)
-    fin[...] = total.astype(BF)
-    out_ref[2 + zlo // 2, place, :] = total.astype(BF)
+
+    def arrived(c):
+        pltpu.make_async_remote_copy(
+            src_ref=zs.at[0, 0], dst_ref=c[0], send_sem=asem.at[0], recv_sem=c[1],
+            device_id=dev(dcore=1), device_id_type=MESH,
+        ).wait_recv()
+
+    place = pl.ds(pl.multiple_of(y * 32, 32), 32)
     last = []
-    for f in (2, 1, 3, 0):
-        for m in (3, 2, 1, 0):
-            if (f, m) != (0, 0):
-                last.append(
-                    started(
-                        make(
-                            fin, out_ref.at[2 + zlo // 2, place, :],
-                            osem.at[f * 4 + m], orsem.at[f * 4 + m], dev(dy=f, dzlo=m),
-                        )
-                    )
-                )
-    for c in last:
-        c.wait_recv()
+    for k in range(4):
+        for f in (2, 1, 3, 0):
+            only = owner if f else jnp.logical_and(owner, zlo != k)
+            c = make(
+                fin, out_ref.at[2 + zlo % 2, place, :], osem.at[k * 4 + f], orsem.at[f * 2 + zlo % 2],
+                dev(dy=f, dzlo=k + 4 - zlo), only,
+            )
+            last.append((c, only))
+
+    @pl.when(owner)
+    def _():
+        zr[zlo] = zs[0, zlo % 2]
+        for k in range(4):
+
+            @pl.when(zlo != k)
+            def _():
+                arrived((zr.at[k], arsem.at[k]))
+
+        for d in (1, 3, 2):
+
+            @pl.when(feeds[d])
+            def _():
+                for k in range(4):
+                    arrived((zr.at[d * 4 + k], arsem.at[d * 4 + k]))
+
+        total = zr[0].astype(F32)
+        for i in range(1, 16):
+            total = total + zr[i].astype(F32)
+        fin[...] = total.astype(BF)
+        for c, only in last:
+            if only is owner:
+                c.start()
+            else:
+                pl.when(only)(c.start)
+        out_ref[2 + zlo % 2, place, :] = total.astype(BF)
+
+    for o in (0, 1):
+        for f in range(4):
+            rows = pl.ds(pl.multiple_of(((y + 4 - f) % 4) * 32, 32), 32)
+            wait = functools.partial(arrived, (out_ref.at[2 + o, rows, :], orsem.at[f * 2 + o]))
+            if f:
+                wait()
+            else:
+                pl.when(zlo != o)(wait)
+    groups = []
     for c, only in sent:
         if only is None:
             c.wait_send()
-    for only in (*feeds.values(), *has.values()):
+        elif any(o is only for o, _ in groups):
+            next(g for o, g in groups if o is only).append(c)
+        else:
+            groups.append((only, [c]))
+    for only, group in groups:
 
         @pl.when(only)
         def _():
-            for c, o in sent:
-                if o is only:
-                    c.wait_send()
+            for c in group:
+                c.wait_send()
 
 
 def local(query_rows, key_rows, value_rows, out_grad):
@@ -329,13 +407,13 @@
             pltpu.VMEM((4, 2, 2, ROWS, D), BF),
             pltpu.VMEM((4, 2, ROWS, D), BF),
             pltpu.VMEM((4, 2, ROWS, D), BF),
-            pltpu.VMEM((4, 4, 2, 32, D), BF),
-            pltpu.VMEM((4, 4, 16, D), BF),
-            pltpu.VMEM((16, 16, D), BF),
-            pltpu.VMEM((16, D), BF),
-            dma((4,)), dma((3,)), dma((3,)), dma((2,)), dma((3,)), dma((3,)), dma((3, 4)), dma((3, 4)), dma((3,)), dma((3,)),
+            pltpu.VMEM((5, 4, 2, 32, D), BF),
+            pltpu.VMEM((4, 2, 32, D), BF),
+            pltpu.VMEM((16, 32, D), BF),
+            pltpu.VMEM((32, D), BF),
+            dma((4,)), dma((3,)), dma((3,)), dma((6,)), dma((3,)), dma((3,)), dma((3, 4)), dma((3, 4)), dma((4,)), dma((4,)),
             dma((3,)), dma((3,)), dma((3,)), dma((3,)), dma((3,)), dma((3,)),
-            dma((4, 4)), dma((4, 4)), dma((16,)), dma((16,)), dma((16,)), dma((16,)),
+            dma((5, 4)), dma((5, 4)), dma((8,)), dma((16,)), dma((16,)), dma((8,)),
         ],
         compiler_params=pltpu.CompilerParams(
             collective_id=0, has_side_effects=True, vmem_limit_bytes=48 * 2**20

time: 57.3 us -> 54.4 us (0.949)
  Pallas kernels: 54.6 us -> 51.9 us
    pallas_call x1, Pallas kernels: 54.6 us -> 51.9 us  [local(): pl.pallas_call(kernel, out_shape=jax.ShapeDtypeStruct((4, ROWS, D), BF),...]
where the time goes in v3:
time: 54.4 us; the launch traced here: 54.1 us
  Pallas kernels  51.9 us (95%)
  other arithmetic  0.83 us (2%)
  local copies, waits for them, and re-layouts  0.65 us (1%)
  between operations  0.64 us (1%)
    pallas_call x1, Pallas kernels, local(): pl.pallas_call(kernel, out_shape=jax.ShapeDtypeStruct((4, ROWS, D), BF),...  51.9 us

profile of v3, /device:TPU:6, one launch (start us, length us, event | category | flops | bytes accessed | tf_op | source)
XLA Modules:
  0.0 54.1 jit_solution(9154239504851053130)
XLA Ops:
  0.6 0.8 %pad_maximum_fusion.in_ref = bf16[4,128,128]{2,1,0:T(8,128)(2,1)S(1)} fusion(bf16[1,128,128]{2,1,0:T(8,128)(2,1)} %bitcast.12, bf16[1,128,128]{2,1,0:T(8,128)(2,1)} %bitcast.13, bf16[1,128,128]{2,1,0:T(8,128)(2,1)} %bitcast.14, bf16[1,128,128]{2,1,0:T(8,128)(2,1)} %bitcast.15), kind=kLoop, calls=%fused_computation | loop fusion | flops 196608 | bytes 262144 | tf_op jit(solution)/shard_map/stack | solution.py:421
  1.5 51.9 %shard_map.75 = bf16[4,128,128]{2,1,0:T(8,128)(2,1)S(1)} custom-call(bf16[4,128,128]{2,1,0:T(8,128)(2,1)S(1)} %pad_maximum_fusion.in_ref), custom_call_target="tpu_custom_call" | custom-call | tf_op jit(solution)/shard_map/pallas_call | solution.py:389
  53.4 0.7 %slice_bitcast_fusion = (bf16[128,128]{1,0:T(8,128)(2,1)}, bf16[128,128]{1,0:T(8,128)(2,1)}, bf16[128,128]{1,0:T(8,128)(2,1)}, bf16[128,128]{1,0:T(8,128)(2,1)}) fusion(bf16[4,128,128]{2,1,0:T(8,128)(2,1)S(1)} %shard_map.75), kind=kLoop, calls=%fused_computation.1 | loop fusion | bytes 262144 | tf_op jit(solution)/shard_map/squeeze | solution.py:422

commit v4 on v3

--- a/solution.py
+++ b/solution.py
@@ -122,21 +122,45 @@
         jnp.int32, (ROWS, ROWS), 0
     )
 
-    def forward(d):
-        queries = qall[...].reshape(4 * ROWS, D)
+    def limit(e, r):
+        return (((x + e) % 4 - x) * 2 + core - (core + r) % 2) * ROWS
+
+    def forward(d, first=0, count=4):
+        queries = qall[first : first + count].reshape(count * ROWS, D)
         keys = kv[d, :, 0].reshape(2 * ROWS, D)
         values = kv[d, :, 1].reshape(2 * ROWS, D)
         products = dot_last(queries, keys)
+        if d == 0:
+            products = jnp.concatenate(
+                [
+                    jnp.concatenate(
+                        [
+                            jnp.where(
+                                gap <= limit(e, r),
+                                products[e * ROWS : (e + 1) * ROWS, r * ROWS : (r + 1) * ROWS],
+                                0.0,
+                            )
+                            for r in range(2)
+                        ],
+                        axis=1,
+                    )
+                    for e in range(4)
+                ],
+                axis=0,
+            )
+        return dot((products * products).astype(BF), values)
+
+    def keep(d):
+        queries = qall[...].reshape(4 * ROWS, D)
+        keys = kv[d, :, 0].reshape(2 * ROWS, D)
+        products = dot_last(keys, queries)
         for e in range(4):
-            block = (zhi * 4 + (x + e) % 4) * 2 + core
             for r in range(2):
-                other = (((zhi + 4 - d) % 4) * 4 + x) * 2 + (core + r) % 2
-                tile = products[e * ROWS : (e + 1) * ROWS, r * ROWS : (r + 1) * ROWS]
+                tile = products[r * ROWS : (r + 1) * ROWS, e * ROWS : (e + 1) * ROWS]
                 if d == 0:
-                    tile = jnp.where(gap <= (block - other) * ROWS, tile, 0.0)
-                s_ref[d, pl.ds(e * ROWS, ROWS), pl.ds(r * ROWS, ROWS)] = tile
-                w_ref[d, pl.ds(e * ROWS, ROWS), pl.ds(r * ROWS, ROWS)] = (tile * tile).astype(BF)
-        return dot(w_ref[d], values)
+                    tile = jnp.where(-gap <= limit(e, r), tile, 0.0)
+                s_ref[d, pl.ds(r * ROWS, ROWS), pl.ds(e * ROWS, ROWS)] = 2.0 * tile
+                w_ref[d, pl.ds(r * ROWS, ROWS), pl.ds(e * ROWS, ROWS)] = (tile * tile).astype(BF)
 
     passed, from_y = {}, {}
     for d in (1, 3):
@@ -193,15 +217,24 @@
     def _():
         for c in from_y[2]:
             c.wait_recv()
+
+
+    arrivals = []
+
+    @pl.when(has[2])
+    def _():
         part[...] += forward(2)
 
-
-    arrivals = []
     for e in (2, 1, 3):
-        parts[e - 1] = part[pl.ds(e * ROWS, ROWS), :].astype(BF)
-        arrivals.append(
-            started(make(parts.at[e - 1], partr.at[e - 1], nsem.at[e - 1], nrsem.at[e - 1], dev(dx=e)))
-        )
+        if e:
+            parts[e - 1] = part[pl.ds(e * ROWS, ROWS), :].astype(BF)
+            arrivals.append(
+                started(
+                    make(parts.at[e - 1], partr.at[e - 1], nsem.at[e - 1], nrsem.at[e - 1], dev(dx=e))
+                )
+            )
+    pl.when(has[2])(functools.partial(keep, 2))
+    pl.when(has[3])(functools.partial(keep, 3))
     for c in arrivals:
         c.wait_recv()
     numerator = part[pl.ds(0, ROWS), :]
@@ -216,6 +249,8 @@
         for e in (2, 1, 3)
     ]
     out_ref[0] = normed.astype(BF)
+    pl.when(has[1])(functools.partial(keep, 1))
+    keep(0)
     for c in from_x:
         c.wait_recv()
 
@@ -248,12 +283,12 @@
             grads = ngall[...].reshape(4 * ROWS, D)
             keys = kv[d, :, 0].reshape(2 * ROWS, D)
             values = kv[d, :, 1].reshape(2 * ROWS, D)
-            coefficient = (2.0 * s_ref[d] * dot_last(grads, values)).astype(BF)
-            dkvs[d, :, 0] = dot_first(coefficient, queries).astype(BF).reshape(2, ROWS, D)
-            dkvs[d, :, 1] = dot_first(w_ref[d], grads).astype(BF).reshape(2, ROWS, D)
+            coefficient = (s_ref[d] * dot_last(values, grads)).astype(BF)
+            dkvs[d, :, 0] = dot(coefficient, queries).astype(BF).reshape(2, ROWS, D)
+            dkvs[d, :, 1] = dot(w_ref[d], grads).astype(BF).reshape(2, ROWS, D)
             for c in from_y[2] if d == 2 else (passed[d],):
                 c.start()
-            dqacc[...] += dot(coefficient, keys)
+            dqacc[...] += dot_first(coefficient, keys)
 
     def over_y(d):
         @pl.when(has[d])
@@ -396,8 +431,8 @@
             pltpu.VMEM((4, ROWS, D), BF),
             pltpu.VMEM((ROWS, D), BF),
             pltpu.VMEM((4, 2, 2, ROWS, D), BF),
-            pltpu.VMEM((4, 4 * ROWS, 2 * ROWS), F32),
-            pltpu.VMEM((4, 4 * ROWS, 2 * ROWS), BF),
+            pltpu.VMEM((4, 2 * ROWS, 4 * ROWS), F32),
+            pltpu.VMEM((4, 2 * ROWS, 4 * ROWS), BF),
             pltpu.VMEM((4 * ROWS, D), F32),
             pltpu.VMEM((3, ROWS, D), BF),
             pltpu.VMEM((3, ROWS, D), BF),

time: 54.4 us -> 54.1 us (level)
  no operation moved by 1% of the time
where the time goes in v4:
time: 54.1 us; the launch traced here: 53.8 us
  Pallas kernels  51.7 us (96%)
  other arithmetic  0.83 us (2%)
  local copies, waits for them, and re-layouts  0.65 us (1%)
  between operations  0.64 us (1%)
    pallas_call x1, Pallas kernels, local(): pl.pallas_call(kernel, out_shape=jax.ShapeDtypeStruct((4, ROWS, D), BF),...  51.7 us

profile of v4, /device:TPU:6, one launch (start us, length us, event | category | flops | bytes accessed | tf_op | source)
XLA Modules:
  0.0 53.8 jit_solution(15405623861956996841)
XLA Ops:
  0.6 0.8 %pad_maximum_fusion.in_ref = bf16[4,128,128]{2,1,0:T(8,128)(2,1)S(1)} fusion(bf16[1,128,128]{2,1,0:T(8,128)(2,1)} %bitcast.12, bf16[1,128,128]{2,1,0:T(8,128)(2,1)} %bitcast.13, bf16[1,128,128]{2,1,0:T(8,128)(2,1)} %bitcast.14, bf16[1,128,128]{2,1,0:T(8,128)(2,1)} %bitcast.15), kind=kLoop, calls=%fused_computation | loop fusion | flops 196608 | bytes 262144 | tf_op jit(solution)/shard_map/stack | solution.py:456
  1.5 51.7 %shard_map.75 = bf16[4,128,128]{2,1,0:T(8,128)(2,1)S(1)} custom-call(bf16[4,128,128]{2,1,0:T(8,128)(2,1)S(1)} %pad_maximum_fusion.in_ref), custom_call_target="tpu_custom_call" | custom-call | tf_op jit(solution)/shard_map/pallas_call | solution.py:424
  53.1 0.7 %slice_bitcast_fusion = (bf16[128,128]{1,0:T(8,128)(2,1)}, bf16[128,128]{1,0:T(8,128)(2,1)}, bf16[128,128]{1,0:T(8,128)(2,1)}, bf16[128,128]{1,0:T(8,128)(2,1)}) fusion(bf16[4,128,128]{2,1,0:T(8,128)(2,1)S(1)} %shard_map.75), kind=kLoop, calls=%fused_computation.1 | loop fusion | bytes 262144 | tf_op jit(solution)/shard_map/squeeze | solution.py:457

commit v5 on v4

--- a/solution.py
+++ b/solution.py
@@ -157,8 +157,7 @@
         for e in range(4):
             for r in range(2):
                 tile = products[r * ROWS : (r + 1) * ROWS, e * ROWS : (e + 1) * ROWS]
-                if d == 0:
-                    tile = jnp.where(-gap <= limit(e, r), tile, 0.0)
+                tile = jnp.where(-gap <= limit(e, r) + d * (8 * ROWS), tile, 0.0)
                 s_ref[d, pl.ds(r * ROWS, ROWS), pl.ds(e * ROWS, ROWS)] = 2.0 * tile
                 w_ref[d, pl.ds(r * ROWS, ROWS), pl.ds(e * ROWS, ROWS)] = (tile * tile).astype(BF)
 
@@ -233,8 +232,7 @@
                     make(parts.at[e - 1], partr.at[e - 1], nsem.at[e - 1], nrsem.at[e - 1], dev(dx=e))
                 )
             )
-    pl.when(has[2])(functools.partial(keep, 2))
-    pl.when(has[3])(functools.partial(keep, 3))
+    lax.fori_loop(1, zhi + 1, lambda d, _: (keep(d), 0)[1], 0)
     for c in arrivals:
         c.wait_recv()
     numerator = part[pl.ds(0, ROWS), :]
@@ -249,7 +247,6 @@
         for e in (2, 1, 3)
     ]
     out_ref[0] = normed.astype(BF)
-    pl.when(has[1])(functools.partial(keep, 1))
     keep(0)
     for c in from_x:
         c.wait_recv()

time: 54.1 us -> 54.1 us (level)
  no operation moved by 1% of the time
where the time goes in v5:
time: 54.1 us; the launch traced here: 53.8 us
  Pallas kernels  51.7 us (96%)
  other arithmetic  0.83 us (2%)
  local copies, waits for them, and re-layouts  0.65 us (1%)
  between operations  0.64 us (1%)
    pallas_call x1, Pallas kernels, local(): pl.pallas_call(kernel, out_shape=jax.ShapeDtypeStruct((4, ROWS, D), BF),...  51.7 us

profile of v5, /device:TPU:6, one launch (start us, length us, event | category | flops | bytes accessed | tf_op | source)
XLA Modules:
  0.0 53.8 jit_solution(11982812445899613440)
XLA Ops:
  0.6 0.8 %pad_maximum_fusion.in_ref = bf16[4,128,128]{2,1,0:T(8,128)(2,1)S(1)} fusion(bf16[1,128,128]{2,1,0:T(8,128)(2,1)} %bitcast.12, bf16[1,128,128]{2,1,0:T(8,128)(2,1)} %bitcast.13, bf16[1,128,128]{2,1,0:T(8,128)(2,1)} %bitcast.14, bf16[1,128,128]{2,1,0:T(8,128)(2,1)} %bitcast.15), kind=kLoop, calls=%fused_computation | loop fusion | flops 196608 | bytes 262144 | tf_op jit(solution)/shard_map/stack | solution.py:453
  1.5 51.7 %shard_map.75 = bf16[4,128,128]{2,1,0:T(8,128)(2,1)S(1)} custom-call(bf16[4,128,128]{2,1,0:T(8,128)(2,1)S(1)} %pad_maximum_fusion.in_ref), custom_call_target="tpu_custom_call" | custom-call | tf_op jit(solution)/shard_map/pallas_call | solution.py:421
  53.1 0.7 %slice_bitcast_fusion = (bf16[128,128]{1,0:T(8,128)(2,1)}, bf16[128,128]{1,0:T(8,128)(2,1)}, bf16[128,128]{1,0:T(8,128)(2,1)}, bf16[128,128]{1,0:T(8,128)(2,1)}) fusion(bf16[4,128,128]{2,1,0:T(8,128)(2,1)S(1)} %shard_map.75), kind=kLoop, calls=%fused_computation.1 | loop fusion | bytes 262144 | tf_op jit(solution)/shard_map/squeeze | solution.py:454
